TPU v7x, 32 devices: a whole 2x2x4 slice. The times are simulated.
32 devices in a mesh: seq: 8 (over z, core), tensor: 4 (over y, x).
Axes of the slice: x: 2, y: 2, z: 4, core: 2. Of those that a mesh axis runs over, the one named last changes fastest.
Arguments:
- qkv: bfloat16 [3, 2048, 8192], P(None, 'seq', 'tensor'), may hold values from -6 to 6
- conv_weight: float32 [3, 3, 8192], P(None, None, 'tensor'), may hold values from -3.6 to 3.6
- decay_rate: float32 [16, 8192], P(None, 'tensor'), may hold values from 1e-05 to 0.06
- residue: float32 [16, 8192], P(None, 'tensor'), may hold values from -3 to 3
- skip_gain: float32 [8192], P('tensor'), may hold values from -5 to 5
- out_weight: bfloat16 [8192, 8192], P('seq', 'tensor'), may hold values from -0.09375 to 0.09375
Outputs:
- mixer_out: bfloat16 [2048, 8192], P('seq', 'tensor')
All inputs are finite; a program needn't handle non-finite values.
Results may differ from a plain program's by a relative error of at most 0.0049.
Values may be sent and summed in bfloat16 or wider, within the bound.
A program may use at most 128 MiB of HBM per device.

v0:
```python
from functools import partial

import jax
import jax.numpy as jnp
from jax import lax
from jax.sharding import PartitionSpec as P

KS = 3


PRECISE = lax.Precision.HIGHEST


def passed_along(block, axis, distance):
    devices = range(lax.axis_size(axis))
    route = [(i - distance, i) for i in devices if i - distance in devices]
    return lax.ppermute(block, axis, route)


def prefix_2(part, axis, combine, identity):
    place = lax.axis_index(axis)
    gathered = jax.tree.map(lambda a: lax.all_gather(a, axis), part)
    state = jax.tree.map(lambda a, e: jnp.zeros_like(a) + jnp.asarray(e, a.dtype), part, identity)

    def one(step, state):
        return combine(
            state, jax.tree.map(lambda a: lax.dynamic_index_in_dim(a, step, 0, False), gathered)
        )

    return lax.fori_loop(0, place, one, state)


def mode_tables(rate_block, residue_block, length):
    lag_values = jnp.arange(length, dtype=jnp.float32)
    decay_table = jnp.exp(-rate_block[:, None, :] * lag_values[None, :, None])
    mode_weight = residue_block * jnp.sqrt(-jnp.expm1(-2.0 * rate_block))
    return (decay_table, mode_weight)


def toeplitz(filter_taps):
    length = filter_taps.shape[0]
    lag_index = jnp.arange(length)[:, None] - jnp.arange(length)[None, :]
    picked = filter_taps[jnp.maximum(lag_index, 0), :]
    return jnp.where(lag_index[:, :, None] >= 0, picked, 0.0)


def inner_block(block_len, inputs):
    x_block, rate_block, residue_block = inputs
    decay_table, mode_weight = mode_tables(rate_block, residue_block, block_len)
    filter_taps = jnp.einsum("mc,mdc->dc", mode_weight, decay_table, precision=PRECISE)
    inner_part = jnp.einsum("tsc,nsc->ntc", toeplitz(filter_taps), x_block, precision=PRECISE)
    local_state = jnp.einsum("msc,nsc->nmc", decay_table[:, ::-1, :], x_block, precision=PRECISE)
    block_decay = jnp.exp(-rate_block * block_len)

    def advance(state, segment):
        return (state * block_decay + segment, state)

    section_state, entering = lax.scan(
        advance, jnp.zeros(rate_block.shape, jnp.float32), local_state
    )
    return (inner_part, entering, section_state)


def carry_block(block_len, inputs):
    rate_block, residue_block, block_entering, section_entering = inputs
    decay_table, mode_weight = mode_tables(rate_block, residue_block, block_len)
    block_ids = jnp.arange(block_entering.shape[0], dtype=jnp.float32)
    reach_back = jnp.exp(-rate_block[None] * (block_len * block_ids)[:, None, None])
    entering_all = block_entering + reach_back * section_entering[None]
    later_table = decay_table * jnp.exp(-rate_block)[:, None, :]
    return jnp.einsum("mc,mdc,nmc->ndc", mode_weight, later_table, entering_all, precision=PRECISE)


def combine_modes(earlier, later):
    return (earlier[0] * later[0], earlier[1] * later[0] + later[1])


def local(qkv, conv_weight, decay_rate, residue, skip_gain, out_weight):
    tokens_here = qkv.shape[1]
    channels = qkv.shape[2]
    modes = decay_rate.shape[0]
    tail_rows = qkv[:, tokens_here - (KS - 1) :, :]
    previous = passed_along(tail_rows, "seq", 1)
    extended = jnp.concatenate([previous, qkv], axis=1).astype(jnp.float32)
    filtered = jnp.zeros((3, tokens_here, channels), jnp.float32)
    for offset in range(KS):
        start_row = KS - 1 - offset
        filtered = (
            filtered
            + conv_weight[:, offset, None, :] * extended[:, start_row : start_row + tokens_here, :]
        )
    product = filtered[1] * filtered[2]
    group_width = min(channels, 128)
    groups = channels // group_width
    block_len = min(tokens_here, 64)
    block_count = tokens_here // block_len
    x_groups = product.reshape(block_count, block_len, groups, group_width).transpose(2, 0, 1, 3)
    rate_groups = decay_rate.reshape(modes, groups, group_width).transpose(1, 0, 2)
    residue_groups = residue.reshape(modes, groups, group_width).transpose(1, 0, 2)
    inner_part, block_entering, section_state = lax.map(
        partial(inner_block, block_len), (x_groups, rate_groups, residue_groups)
    )
    section_state = section_state.transpose(1, 0, 2).reshape(modes, channels)
    section_decay = jnp.exp(-decay_rate * tokens_here)
    identity = (
        jnp.ones(section_state.shape, jnp.float32),
        jnp.zeros(section_state.shape, jnp.float32),
    )
    prefix = prefix_2((section_decay, section_state), "seq", combine_modes, identity)
    section_entering = prefix[1].reshape(modes, groups, group_width).transpose(1, 0, 2)
    carried = lax.map(
        partial(carry_block, block_len),
        (rate_groups, residue_groups, block_entering, section_entering),
    )
    long_part = (inner_part + carried).transpose(1, 2, 0, 3).reshape(tokens_here, channels)
    long_part = long_part + skip_gain[None, :] * product
    mixed_local = (filtered[0] * long_part).astype(jnp.bfloat16)
    features = lax.all_gather(mixed_local, "tensor", axis=1, tiled=True)
    projected = jnp.dot(
        features,
        lax.all_gather(out_weight, "seq", axis=0, tiled=True),
        preferred_element_type=jnp.float32,
    )
    return projected.astype(jnp.bfloat16)


def solution(mesh):
    return jax.shard_map(
        local,
        mesh=mesh,
        in_specs=(
            P(None, "seq", "tensor"),
            P(None, None, "tensor"),
            P(None, "tensor"),
            P(None, "tensor"),
            P("tensor"),
            P("seq", "tensor"),
        ),
        out_specs=P("seq", "tensor"),
        check_vma=False,
    )
```

profile of v0, /device:TPU:0, one launch (start us, length us, event | category | flops | bytes accessed | tf_op | source)
XLA Modules:
  0.0 1033.1 jit_solution(2310587772206397896)
XLA Ops:
  28.3 516.9 %while.50 = (s32[]{:T(128)}, f32[16,4,64,128]{2,1,3,0:T(4,128)}, f32[16,4,16,128]{3,2,1,0:T(8,128)}, f32[16,16,128]{2,1,0:T(8,128)}, f32[16,4,64,128]{3,0,2,1:T(...) while((s32[]{:T(128)}, f32[16,4,64,128]{2,1,3,0:T(4,128)}, ...), condition=%wide.region_3.4_spmd, body=%wide.region_0.3_spmd.sunk | while | flops 32536580 | bytes 17319760 | solution.py:100
  36.2 10.8 %gather_fusion = f32[4096,128]{1,0:T(8,128)S(1)} fusion(f32[64,128]{1,0:T(8,128)S(1)} %bitcast.140, s32[4096]{0:T(1024)S(1)} %broadcast_clamp_fusion.2), kind=kCustom, calls=%fused_computation.clone.1 | custom fusion | bytes 4210688 | tf_op jit(solution)/shard_map/while/body/eval_jaxpr/gather | solution.py:43
  47.0 4.6 copy.71
  51.6 9.0 fusion.53
  68.6 10.8 %gather_fusion = f32[4096,128]{1,0:T(8,128)S(1)} fusion(f32[64,128]{1,0:T(8,128)S(1)} %bitcast.140, s32[4096]{0:T(1024)S(1)} %broadcast_clamp_fusion.2), kind=kCustom, calls=%fused_computation.clone.1 | custom fusion | bytes 4210688 | tf_op jit(solution)/shard_map/while/body/eval_jaxpr/gather | solution.py:43
  79.3 4.6 copy.71
  83.9 9.0 fusion.53
  100.8 10.8 %gather_fusion = f32[4096,128]{1,0:T(8,128)S(1)} fusion(f32[64,128]{1,0:T(8,128)S(1)} %bitcast.140, s32[4096]{0:T(1024)S(1)} %broadcast_clamp_fusion.2), kind=kCustom, calls=%fused_computation.clone.1 | custom fusion | bytes 4210688 | tf_op jit(solution)/shard_map/while/body/eval_jaxpr/gather | solution.py:43
  111.6 4.6 copy.71
  116.2 9.0 fusion.53
  133.2 10.8 %gather_fusion = f32[4096,128]{1,0:T(8,128)S(1)} fusion(f32[64,128]{1,0:T(8,128)S(1)} %bitcast.140, s32[4096]{0:T(1024)S(1)} %broadcast_clamp_fusion.2), kind=kCustom, calls=%fused_computation.clone.1 | custom fusion | bytes 4210688 | tf_op jit(solution)/shard_map/while/body/eval_jaxpr/gather | solution.py:43
  143.9 4.6 copy.71
  148.5 9.0 fusion.53
  165.5 10.8 %gather_fusion = f32[4096,128]{1,0:T(8,128)S(1)} fusion(f32[64,128]{1,0:T(8,128)S(1)} %bitcast.140, s32[4096]{0:T(1024)S(1)} %broadcast_clamp_fusion.2), kind=kCustom, calls=%fused_computation.clone.1 | custom fusion | bytes 4210688 | tf_op jit(solution)/shard_map/while/body/eval_jaxpr/gather | solution.py:43
  176.2 4.6 copy.71
  180.8 9.0 fusion.53
  197.8 10.8 %gather_fusion = f32[4096,128]{1,0:T(8,128)S(1)} fusion(f32[64,128]{1,0:T(8,128)S(1)} %bitcast.140, s32[4096]{0:T(1024)S(1)} %broadcast_clamp_fusion.2), kind=kCustom, calls=%fused_computation.clone.1 | custom fusion | bytes 4210688 | tf_op jit(solution)/shard_map/while/body/eval_jaxpr/gather | solution.py:43
  208.5 4.6 copy.71
  213.1 9.0 fusion.53
  230.1 10.8 %gather_fusion = f32[4096,128]{1,0:T(8,128)S(1)} fusion(f32[64,128]{1,0:T(8,128)S(1)} %bitcast.140, s32[4096]{0:T(1024)S(1)} %broadcast_clamp_fusion.2), kind=kCustom, calls=%fused_computation.clone.1 | custom fusion | bytes 4210688 | tf_op jit(solution)/shard_map/while/body/eval_jaxpr/gather | solution.py:43
  240.8 4.6 copy.71
  245.4 9.1 fusion.53
  262.4 10.8 %gather_fusion = f32[4096,128]{1,0:T(8,128)S(1)} fusion(f32[64,128]{1,0:T(8,128)S(1)} %bitcast.140, s32[4096]{0:T(1024)S(1)} %broadcast_clamp_fusion.2), kind=kCustom, calls=%fused_computation.clone.1 | custom fusion | bytes 4210688 | tf_op jit(solution)/shard_map/while/body/eval_jaxpr/gather | solution.py:43
  273.2 4.6 copy.71
  277.7 9.0 fusion.53
  294.7 10.8 %gather_fusion = f32[4096,128]{1,0:T(8,128)S(1)} fusion(f32[64,128]{1,0:T(8,128)S(1)} %bitcast.140, s32[4096]{0:T(1024)S(1)} %broadcast_clamp_fusion.2), kind=kCustom, calls=%fused_computation.clone.1 | custom fusion | bytes 4210688 | tf_op jit(solution)/shard_map/while/body/eval_jaxpr/gather | solution.py:43
  310.0 9.0 fusion.53
  327.0 10.8 %gather_fusion = f32[4096,128]{1,0:T(8,128)S(1)} fusion(f32[64,128]{1,0:T(8,128)S(1)} %bitcast.140, s32[4096]{0:T(1024)S(1)} %broadcast_clamp_fusion.2), kind=kCustom, calls=%fused_computation.clone.1 | custom fusion | bytes 4210688 | tf_op jit(solution)/shard_map/while/body/eval_jaxpr/gather | solution.py:43
  342.3 9.1 fusion.53
  359.3 10.8 %gather_fusion = f32[4096,128]{1,0:T(8,128)S(1)} fusion(f32[64,128]{1,0:T(8,128)S(1)} %bitcast.140, s32[4096]{0:T(1024)S(1)} %broadcast_clamp_fusion.2), kind=kCustom, calls=%fused_computation.clone.1 | custom fusion | bytes 4210688 | tf_op jit(solution)/shard_map/while/body/eval_jaxpr/gather | solution.py:43
  374.6 9.0 fusion.53
  391.6 10.8 %gather_fusion = f32[4096,128]{1,0:T(8,128)S(1)} fusion(f32[64,128]{1,0:T(8,128)S(1)} %bitcast.140, s32[4096]{0:T(1024)S(1)} %broadcast_clamp_fusion.2), kind=kCustom, calls=%fused_computation.clone.1 | custom fusion | bytes 4210688 | tf_op jit(solution)/shard_map/while/body/eval_jaxpr/gather | solution.py:43
  407.0 9.0 fusion.53
  423.9 10.8 %gather_fusion = f32[4096,128]{1,0:T(8,128)S(1)} fusion(f32[64,128]{1,0:T(8,128)S(1)} %bitcast.140, s32[4096]{0:T(1024)S(1)} %broadcast_clamp_fusion.2), kind=kCustom, calls=%fused_computation.clone.1 | custom fusion | bytes 4210688 | tf_op jit(solution)/shard_map/while/body/eval_jaxpr/gather | solution.py:43
  439.3 9.0 fusion.53
  456.2 10.8 %gather_fusion = f32[4096,128]{1,0:T(8,128)S(1)} fusion(f32[64,128]{1,0:T(8,128)S(1)} %bitcast.140, s32[4096]{0:T(1024)S(1)} %broadcast_clamp_fusion.2), kind=kCustom, calls=%fused_computation.clone.1 | custom fusion | bytes 4210688 | tf_op jit(solution)/shard_map/while/body/eval_jaxpr/gather | solution.py:43
  471.6 9.0 fusion.53
  488.5 10.8 %gather_fusion = f32[4096,128]{1,0:T(8,128)S(1)} fusion(f32[64,128]{1,0:T(8,128)S(1)} %bitcast.140, s32[4096]{0:T(1024)S(1)} %broadcast_clamp_fusion.2), kind=kCustom, calls=%fused_computation.clone.1 | custom fusion | bytes 4210688 | tf_op jit(solution)/shard_map/while/body/eval_jaxpr/gather | solution.py:43
  503.9 9.0 fusion.53
  520.9 10.8 %gather_fusion = f32[4096,128]{1,0:T(8,128)S(1)} fusion(f32[64,128]{1,0:T(8,128)S(1)} %bitcast.140, s32[4096]{0:T(1024)S(1)} %broadcast_clamp_fusion.2), kind=kCustom, calls=%fused_computation.clone.1 | custom fusion | bytes 4210688 | tf_op jit(solution)/shard_map/while/body/eval_jaxpr/gather | solution.py:43
  536.2 9.0 fusion.53
  547.0 24.8 %all-gather.6.cloned.1.call-done = f32[8,16,2048]{2,1,0:T(8,128)} async-done(((f32[1,16,2048]{2,1,0:T(8,128)}), f32[8,16,2048]{2,1,0:T(8,128)}) %all-gather.6.cloned.1.call-update) | async-done | bytes 1048592 | tf_op jit(solution)/shard_map/all_gather | solution.py:22
  575.3 66.5 %while.52 = (s32[]{:T(128)}, f32[16,4,64,128]{2,1,3,0:T(4,128)}, f32[16,4,16,128]{3,2,1,0:T(8,128)}, f32[16,16,128]{1,2,0:T(8,128)S(1)}, f32[16,16,128]{1,2,0:T(8,128)S(1)}, /*index=5*/f32[16,16,128]{1,2,0:T(8,128)}, s32[]{:T(128)}) while((s32[]{:T(128)}, f32[16,4,64,128]{2,1,3,0:T(4,128)}, f32[16,4,16,128]{3,2,1,0:T(8,128)}, ...), condition=%wide.region_7.8_spmd, body=%wide.region_6.7_spmd.sunk | while | flops 6594566 | bytes 1049705 | solution.py:111
  641.7 6.7 add_bitcast_fusion
  654.5 5.3 fusion.32
  660.4 59.0 %all-gather.8.cloned.1.call-done = bf16[256,8192]{1,0:T(8,128)(2,1)} async-done(((bf16[256,2048]{1,0:T(8,128)(2,1)}), bf16[256,8192]{1,0:T(8,128)(2,1)}) %all-gather.8.cloned.1.call-update) | async-done | bytes 4194320 | tf_op jit(solution)/shard_map/all_gather | solution.py:118
  719.4 290.1 %all-gather.10.cloned.1.call-done = bf16[8192,2048]{1,0:T(8,128)(2,1)} async-done(((bf16[1024,2048]{1,0:T(8,128)(2,1)}), bf16[8192,2048]{1,0:T(8,128)(2,1)}) %all-gather.10.cloned.1.call-update) | async-done | bytes 33554448 | tf_op jit(solution)/shard_map/all_gather | solution.py:121
  1009.5 17.0 %convolution_convert_fusion = bf16[256,2048]{1,0:T(8,128)(2,1)} fusion(bf16[256,8192]{1,0:T(8,128)(2,1)} %all-gather.8.cloned.1.call-done, bf16[8192,2048]{1,0:T(8,128)(2,1)} %all-gather.10.cloned.1.call-done), kind=kOutput, calls=%fused_computation.55 | convolution fusion | flops 8590458880 | bytes 38797312 | tf_op jit(solution)/shard_map/dot_general | solution.py:119
  (674 shorter events, 263.1 us)
Async XLA Ops:
  6.5 540.5 %all-gather.12.cloned.1.call-start = ((), (), s32[]{:S(2)}) async-start(), calls=%async_computation.3 | async-start | bytes 1179648 | tf_op jit(solution)/shard_map/all_gather | solution.py:22
  7.5 9.0 collective-permute-start
  11.4 560.3 %all-gather.6.cloned.1.call-start = ((), (), s32[]{:S(2)}) async-start(), calls=%async_computation | async-start | bytes 1179648 | tf_op jit(solution)/shard_map/all_gather | solution.py:22
  15.5 3.9 copy-start.1
  21.2 2.7 copy-start
  28.3 0.6 copy-start.2
  51.6 9.1 copy-start.3
  60.6 0.7 copy-start.2
  83.9 9.1 copy-start.3
  92.9 0.7 copy-start.2
  116.2 9.1 copy-start.3
  125.2 0.7 copy-start.2
  148.5 9.1 copy-start.3
  157.6 0.7 copy-start.2
  180.8 9.1 copy-start.3
  189.9 0.7 copy-start.2
  213.1 9.1 copy-start.3
  222.1 0.7 copy-start.2
  245.4 9.1 copy-start.3
  254.5 0.7 copy-start.2
  277.7 9.0 copy-start.3
  286.8 0.7 copy-start.2
  310.0 9.1 copy-start.3
  319.1 0.7 copy-start.2
  342.3 9.1 copy-start.3
  351.4 0.7 copy-start.2
  374.6 9.1 copy-start.3
  383.7 0.7 copy-start.2
  406.9 9.1 copy-start.3
  416.0 0.7 copy-start.2
  439.2 9.1 copy-start.3
  448.3 0.7 copy-start.2
  471.6 9.1 copy-start.3
  480.6 0.7 copy-start.2
  503.9 9.1 copy-start.3
  512.9 0.7 copy-start.2
  536.2 9.1 copy-start.3
  546.9 172.5 %all-gather.8.cloned.1.call-start = ((), (), s32[]{:S(2)}) async-start(), calls=%async_computation.1 | async-start | bytes 5242880 | tf_op jit(solution)/shard_map/all_gather | solution.py:118
  648.4 6.1 copy-start.4
  659.8 349.7 %all-gather.10.cloned.1.call-start = ((), (), s32[]{:S(2)}) async-start(), calls=%async_computation.2 | async-start | bytes 37748736 | tf_op jit(solution)/shard_map/all_gather | solution.py:121
Sparse Core Ops, SparseCore 0:
  11.6 24.6 all-gather.11
  547.0 24.6 all-gather.5
  660.0 59.4 all-gather.7
  720.9 288.6 all-gather.9
where the time goes:
time: 1040 us; the launch traced here: 1030 us
  waiting for transfers between devices  374 us (36%)
  local copies, waits for them, and re-layouts  350 us (34%)
  matrix products  226 us (22%)
  other arithmetic  62.7 us (6%)
  between operations  13.3 us (1%)
    all_gather x1, waiting for transfers between devices, local(): lax.all_gather(out_weight, 'seq', axis=0, tiled=True)  290 us
    gather x32, local copies, waits for them, and re-layouts, toeplitz(): picked = filter_taps[jnp.maximum(lag_index, 0), :]  245 us
    dot_general x16, matrix products, inner_block(): jnp.einsum('tsc,nsc->ntc', toeplitz(filter_taps), x_block, precision=PREC...  145 us
    all_gather x1, waiting for transfers between devices, local(): features = lax.all_gather(mixed_local, 'tensor', axis=1, tiled=True)  59 us
    dot_general x16, matrix products, carry_block(): jnp.einsum('mc,mdc,nmc->ndc', mode_weight, later_table, entering_all, pre...  36.7 us
    dot_general x16, matrix products, inner_block(): jnp.einsum('msc,nsc->nmc', decay_table[:, ::-1, :], x_block, precision=PR...  28.1 us
    all_gather x2, waiting for transfers between devices, prefix_2(): gathered = jax.tree.map(lambda a: lax.all_gather(a, axis), part)  24.8 us
    dynamic_slice x32, local copies, waits for them, and re-layouts, local(): lax.map(partial(inner_block, block_len), (x_groups, rate_groups, residue_...  23.6 us
  transfers between devices with their start and end apart: 5, of which 3 were waited for; matrix products, arithmetic and copies ran while one was open for 51% of the time, Pallas kernels for 0%

commit v1 on v0

v1 whole, which is shorter than its diff:
```python
import functools

import jax
import jax.numpy as jnp
from jax import lax
from jax.experimental import pallas as pl
from jax.experimental.pallas import tpu as pltpu
from jax.sharding import PartitionSpec as P

MESH = pl.DeviceIdType.MESH
LANES = 128
HALO = 16


def kernel(
    ns,
    nt,
    modes,
    qkv,
    conv_w,
    decay,
    decay_sec,
    gain,
    skip,
    weight,
    out,
    halo,
    ext,
    prod,
    qf,
    mixed,
    wfull,
    state,
    other,
    total,
    totals,
    enter,
    stage,
    full,
    part,
    recv,
    own,
    halo_sem,
    w_sem,
    swap_sem,
    tot_send,
    tot_recv,
    s1_send,
    s1_recv,
    s2_send,
    s2_recv,
    s3_send,
    s3_recv,
    rs_send,
    rs_recv,
    loc_sem,
):
    nz = ns // 2
    tok = qkv.shape[1]
    ch = qkv.shape[2]
    groups = ch // LANES
    quarter = tok // nt
    rows_w = weight.shape[0]
    cols = weight.shape[1]
    s = lax.axis_index("seq")
    t = lax.axis_index("tensor")
    z = s // 2
    c = s % 2
    mate = 2 * z + (1 - c)

    def dev(seq, ten):
        return (seq, ten)

    barrier = pltpu.get_barrier_semaphore()
    for d in range(1, ns):
        pl.semaphore_signal(barrier, inc=1, device_id=dev((s + d) % ns, t), device_id_type=MESH)
    for d in range(1, nt):
        pl.semaphore_signal(barrier, inc=1, device_id=dev(s, (t + d) % nt), device_id_type=MESH)
    pl.semaphore_wait(barrier, ns - 1 + nt - 1)

    halo_copy = pltpu.make_async_remote_copy(
        src_ref=qkv.at[:, pl.ds(tok - HALO, HALO), :],
        dst_ref=halo,
        send_sem=halo_sem.at[0],
        recv_sem=halo_sem.at[1],
        device_id=dev((s + 1) % ns, t),
        device_id_type=MESH,
    )

    @pl.when(s < ns - 1)
    def _():
        halo_copy.start()

    w_rows = pl.ds(pl.multiple_of(c * rows_w, rows_w), rows_w)
    w_remote = pltpu.make_async_remote_copy(
        src_ref=weight,
        dst_ref=wfull.at[w_rows, :],
        send_sem=w_sem.at[0],
        recv_sem=w_sem.at[1],
        device_id=dev(mate, t),
        device_id_type=MESH,
    )
    w_remote.start()
    w_local = pltpu.make_async_copy(weight, wfull.at[w_rows, :], w_sem.at[2])
    w_local.start()

    @pl.when(s == 0)
    def _():
        halo[...] = jnp.zeros_like(halo)

    @pl.when(s > 0)
    def _():
        halo_copy.wait_recv()

    def short(i, lanes):
        ext[i, 0:HALO, :] = halo[i, :, lanes].astype(jnp.float32)
        ext[i, HALO : HALO + tok, :] = qkv[i, :, lanes].astype(jnp.float32)
        taps = conv_w[pl.ds(3 * i, 3), lanes]
        return (
            taps[0:1] * ext[i, HALO : HALO + tok, :]
            + taps[1:2] * ext[i, HALO - 1 : HALO - 1 + tok, :]
            + taps[2:3] * ext[i, HALO - 2 : HALO - 2 + tok, :]
        )

    for g in range(groups):
        lanes = pl.ds(g * LANES, LANES)
        prod[pl.ds(g, tok, stride=groups), :] = short(1, lanes) * short(2, lanes)

    width = min(8, groups)

    def mode_rows(ref, m, h):
        return ref[m * groups + h * width : m * groups + (h + 1) * width, :]

    def tree(values):
        while len(values) > 1:
            values = [a + b for a, b in zip(values[::2], values[1::2])] + (
                [values[-1]] if len(values) % 2 else []
            )
        return values[0]

    for h in range(groups // width):
        skips = skip[h * width : (h + 1) * width, :]

        def step(i, states, h=h, skips=skips):
            rows = pl.ds(pl.multiple_of(i * groups + h * width, width), width)
            x = prod[rows, :]
            new = tuple(st * mode_rows(decay, m, h) + x for m, st in enumerate(states))
            terms = [st * mode_rows(gain, m, h) for m, st in enumerate(new)]
            prod[rows, :] = tree(terms) + skips * x
            return new

        states = lax.fori_loop(
            0,
            tok,
            step,
            tuple(jnp.zeros((width, LANES), jnp.float32) for _ in range(modes)),
            unroll=4,
        )
        for m in range(modes):
            state[m * groups + h * width : m * groups + (h + 1) * width, :] = states[m]

    swap = pltpu.make_async_remote_copy(
        src_ref=state,
        dst_ref=other,
        send_sem=swap_sem.at[0],
        recv_sem=swap_sem.at[1],
        device_id=dev(mate, t),
        device_id_type=MESH,
    )
    swap.start()
    swap.wait_recv()

    @pl.when(c == 0)
    def _():
        total[...] = (decay_sec[...] * state[...] + other[...]).astype(total.dtype)

    @pl.when(c == 1)
    def _():
        total[...] = (decay_sec[...] * other[...] + state[...]).astype(total.dtype)

    def tot_copy(target, source):
        return pltpu.make_async_remote_copy(
            src_ref=total,
            dst_ref=totals.at[source],
            send_sem=tot_send.at[target],
            recv_sem=tot_recv.at[source],
            device_id=dev(2 * target + c, t),
            device_id_type=MESH,
        )

    for k in range(1, nz):

        @pl.when(k > z)
        def _(k=k):
            tot_copy(k, z).start()

    for g in range(groups):
        lanes = pl.ds(g * LANES, LANES)
        qf[:, lanes] = short(0, lanes)

    enter[...] = jnp.zeros_like(enter)
    for k in range(nz - 1):

        @pl.when(k < z)
        def _(k=k):
            tot_copy(z, k).wait_recv()
            enter[...] = enter[...] * decay_sec[...] * decay_sec[...] + totals[k].astype(
                jnp.float32
            )

    @pl.when(c == 1)
    def _():
        enter[...] = decay_sec[...] * enter[...] + other[...]

    for h in range(groups // width):

        def fix(i, carried, h=h):
            rows = pl.ds(pl.multiple_of(i * groups + h * width, width), width)
            prod[rows, :] = prod[rows, :] + tree(list(carried))
            return tuple(u * mode_rows(decay, m, h) for m, u in enumerate(carried))

        lax.fori_loop(
            0,
            tok,
            fix,
            tuple(
                mode_rows(gain, m, h) * mode_rows(decay, m, h) * mode_rows(enter, m, h)
                for m in range(modes)
            ),
            unroll=4,
        )

    for g in range(groups):
        lanes = pl.ds(g * LANES, LANES)
        mixed[:, lanes] = (qf[:, lanes] * prod[pl.ds(g, tok, stride=groups), :]).astype(
            mixed.dtype
        )

    def share(index):
        return pl.ds(pl.multiple_of(index * quarter, quarter), quarter)

    def s1_copy(target, source):
        return pltpu.make_async_remote_copy(
            src_ref=mixed.at[share(target), :],
            dst_ref=stage.at[source],
            send_sem=s1_send.at[target],
            recv_sem=s1_recv.at[source],
            device_id=dev(s, target),
            device_id_type=MESH,
        )

    def each_peer(body):
        def one(d, carry):
            body((t + d) % nt)
            return carry

        lax.fori_loop(1, nt, one, 0)

    each_peer(lambda q: s1_copy(q, t).start())
    own_copy = pltpu.make_async_copy(mixed.at[share(t), :], stage.at[t], loc_sem.at[0])
    own_copy.start()
    own_copy.wait()
    each_peer(lambda q: s1_copy(t, q).wait_recv())

    def s2_copy(target, source):
        return pltpu.make_async_remote_copy(
            src_ref=stage.at[target],
            dst_ref=full.at[source, share(t), :],
            send_sem=s2_send.at[target],
            recv_sem=s2_recv.at[source],
            device_id=dev(2 * target + c, t),
            device_id_type=MESH,
        )

    candidates = 2 * (nz - 1)

    def each_plane(e, body):
        d = nz - 1 - e // 2
        k = z + d * (1 - 2 * (e % 2))

        @pl.when((k >= 0) & (k < nz))
        def _():
            body(k)

    def loop_planes(body):
        def one(e, carry):
            each_plane(e, body)
            return carry

        lax.fori_loop(0, candidates, one, 0)

    loop_planes(lambda k: s2_copy(k, z).start())
    keep = pltpu.make_async_copy(stage.at[z], full.at[z, share(t), :], loc_sem.at[1])
    keep.start()
    keep.wait()

    def s3_copy(target, source, k):
        rows = full.at[k, share(source), :]
        return pltpu.make_async_remote_copy(
            src_ref=rows,
            dst_ref=rows,
            send_sem=s3_send.at[k, target],
            recv_sem=s3_recv.at[k, source],
            device_id=dev(s, target),
            device_id_type=MESH,
        )

    def spread(k):
        each_peer(lambda q: s3_copy(q, t, k).start())

    def spread_received(k):
        s2_copy(z, k).wait_recv()
        spread(k)

    def gathered(k):
        each_peer(lambda q: s3_copy(t, q, k).wait_recv())

    tile = min(512, cols)

    def product(k, store):
        def one(n, carry):
            lanes = pl.ds(pl.multiple_of(n * tile, tile), tile)
            store(
                lanes,
                jnp.dot(full[k], wfull[:, lanes], preferred_element_type=jnp.float32),
            )
            return carry

        lax.fori_loop(0, cols // tile, one, 0)

    def rs_copy(k, slot, target, source_slot):
        return pltpu.make_async_remote_copy(
            src_ref=part.at[k],
            dst_ref=recv.at[slot],
            send_sem=rs_send.at[k],
            recv_sem=rs_recv.at[slot],
            device_id=dev(2 * target + c, t),
            device_id_type=MESH,
        )

    def rs_wait(slot):
        rs_copy(z, slot, z, slot).wait_recv()

    def contribute(k):
        gathered(k)

        def fresh(lanes, value):
            part[k, :, lanes] = value.astype(part.dtype)

        def added(lanes, value):
            part[k, :, lanes] = (value + recv[k, :, lanes].astype(jnp.float32)).astype(part.dtype)

        @pl.when((k > z) & (z > 0))
        def _():
            rs_wait(k)
            product(k, added)

        @pl.when((k < z) & (z < nz - 1))
        def _():
            rs_wait(k)
            product(k, added)

        @pl.when(((k > z) & (z == 0)) | ((k < z) & (z == nz - 1)))
        def _():
            product(k, fresh)

        @pl.when(k > z)
        def _():
            rs_copy(k, k, z + 1, k).start()

        @pl.when((k < z) & (k < z - 1))
        def _():
            rs_copy(k, k, z - 1, k).start()

        @pl.when((k < z) & (k == z - 1))
        def _():
            rs_copy(k, nz, z - 1, k).start()

    spread(z)
    w_local.wait()
    w_remote.wait_recv()

    lead = 2
    for e in range(lead):
        each_plane(e, spread_received)
    gathered(z)

    def keep_own(lanes, value):
        own[:, lanes] = value

    product(z, keep_own)

    def one_plane(e, carry):
        @pl.when(e + lead < candidates)
        def _():
            each_plane(e + lead, spread_received)

        each_plane(e, contribute)
        return carry

    lax.fori_loop(0, candidates, one_plane, 0)

    @pl.when(z > 0)
    def _():
        rs_wait(z)
        own[...] += recv[z].astype(jnp.float32)

    @pl.when(z < nz - 1)
    def _():
        rs_wait(nz)
        own[...] += recv[nz].astype(jnp.float32)

    out[...] = own[...].astype(out.dtype)

    @pl.when(s < ns - 1)
    def _():
        halo_copy.wait_send()

    w_remote.wait_send()
    swap.wait_send()
    for k in range(1, nz):

        @pl.when(k > z)
        def _(k=k):
            tot_copy(k, z).wait_send()

    each_peer(lambda q: s1_copy(q, t).wait_send())
    loop_planes(lambda k: s2_copy(k, z).wait_send())

    def all_sent(k):
        each_peer(lambda q: s3_copy(q, t, k).wait_send())

    all_sent(z)
    loop_planes(all_sent)
    loop_planes(lambda k: rs_copy(k, k, z, k).wait_send())


def local(ns, nt, qkv, conv_weight, decay_rate, residue, skip_gain, out_weight):
    tok, ch = qkv.shape[1], qkv.shape[2]
    modes = decay_rate.shape[0]
    groups = ch // LANES
    nz = ns // 2
    cols = out_weight.shape[1]
    rows = modes * groups
    decay = jnp.exp(-decay_rate).reshape(rows, LANES)
    decay_sec = jnp.exp(-decay_rate * tok).reshape(rows, LANES)
    gain = (residue * jnp.sqrt(-jnp.expm1(-2.0 * decay_rate))).reshape(rows, LANES)
    vmem = pl.BlockSpec(memory_space=pltpu.VMEM)
    f32, bf16 = jnp.float32, jnp.bfloat16
    dma = pltpu.SemaphoreType.DMA
    return pl.pallas_call(
        functools.partial(kernel, ns, nt, modes),
        out_shape=jax.ShapeDtypeStruct((tok, cols), bf16),
        in_specs=[vmem] * 6 + [pl.BlockSpec(memory_space=pl.ANY)],
        out_specs=vmem,
        scratch_shapes=[
            pltpu.VMEM((3, HALO, ch), bf16),
            pltpu.VMEM((3, HALO + tok, LANES), f32),
            pltpu.VMEM((tok * groups, LANES), f32),
            pltpu.VMEM((tok, ch), f32),
            pltpu.VMEM((tok, ch), bf16),
            pltpu.VMEM((ch, cols), bf16),
            pltpu.VMEM((rows, LANES), f32),
            pltpu.VMEM((rows, LANES), f32),
            pltpu.VMEM((rows, LANES), bf16),
            pltpu.VMEM((nz, rows, LANES), bf16),
            pltpu.VMEM((rows, LANES), f32),
            pltpu.VMEM((nt, tok // nt, ch), bf16),
            pltpu.VMEM((nz, tok, ch), bf16),
            pltpu.VMEM((nz, tok, cols), bf16),
            pltpu.VMEM((nz + 1, tok, cols), bf16),
            pltpu.VMEM((tok, cols), f32),
            dma((2,)),
            dma((3,)),
            dma((2,)),
            dma((nz,)),
            dma((nz,)),
            dma((nt,)),
            dma((nt,)),
            dma((nz,)),
            dma((nz,)),
            dma((nz, nt)),
            dma((nz, nt)),
            dma((nz,)),
            dma((nz + 1,)),
            dma((2,)),
        ],
        compiler_params=pltpu.CompilerParams(
            collective_id=0, has_side_effects=True, vmem_limit_bytes=56 * 1024 * 1024
        ),
        cost_estimate=pl.CostEstimate(
            flops=2 * tok * nz * ch * cols, bytes_accessed=12 * 1024 * 1024, transcendentals=0
        ),
    )(
        qkv,
        conv_weight.reshape(-1, ch),
        decay,
        decay_sec,
        gain,
        skip_gain.reshape(groups, LANES),
        out_weight,
    )


def solution(mesh):
    return jax.shard_map(
        functools.partial(local, mesh.shape["seq"], mesh.shape["tensor"]),
        mesh=mesh,
        in_specs=(
            P(None, "seq", "tensor"),
            P(None, None, "tensor"),
            P(None, "tensor"),
            P(None, "tensor"),
            P("tensor"),
            P("seq", "tensor"),
        ),
        out_specs=P("seq", "tensor"),
        check_vma=False,
    )
```

time: 1040 us -> 157 us (0.15)
  waiting for transfers between devices: 374 us -> 0 us
  local copies, waits for them, and re-layouts: 350 us -> 5.94 us
  matrix products: 226 us -> 0 us
  Pallas kernels: 0 us -> 150 us
  other arithmetic: 62.7 us -> 1.08 us
  between operations: 13.3 us -> 0.01 us
    all_gather x4 -> x0, waiting for transfers between devices: 374 us -> none  [the longest x1 290 us: local(): lax.all_gather(out_weight, 'seq', axis=0, tiled=True)]
    gather x32 -> x0, local copies, waits for them, and re-layouts: 245 us -> none  [toeplitz(): picked = filter_taps[jnp.maximum(lag_index, 0), :]]
    dot_general x49 -> x0, matrix products: 226 us -> none  [the longest x16 145 us: inner_block(): jnp.einsum('tsc,nsc->ntc', toeplitz(filter_taps), x_block, precision=PREC...]
    pallas_call x0 -> x1, Pallas kernels: none -> 150 us  [local(): pl.pallas_call(functools.partial(kernel, ns, nt, modes), out_shape=jax.Sh...]
    dynamic_slice x64 -> x0, local copies, waits for them, and re-layouts: 38.2 us -> none  [the longest x32 23.6 us: local(): lax.map(partial(inner_block, block_len), (x_groups, rate_groups, residue_...]
    while x48 -> x0, other arithmetic: 22 us -> none
    dynamic_update_slice x32 -> x0, local copies, waits for them, and re-layouts: 19.4 us -> none  [local(): lax.map(partial(inner_block, block_len), (x_groups, rate_groups, residue_...]
    while x99 -> x0, local copies, waits for them, and re-layouts: 13.3 us -> none
  transfers between devices with their start and end apart: 5 -> 0, of which waited for: 3 -> 0; matrix products, arithmetic and copies ran while one was open for 51% -> 0% of each run, Pallas kernels for 0% -> 0%
where the time goes in v1:
time: 157 us
  Pallas kernels  150 us (96%)
  local copies, waits for them, and re-layouts  5.94 us (4%)
    pallas_call x1, Pallas kernels, local(): pl.pallas_call(functools.partial(kernel, ns, nt, modes), out_shape=jax.Sh...  150 us

profile of v1, /device:TPU:0, one launch (start us, length us, event | category | flops | bytes accessed | tf_op | source)
XLA Modules:
  0.0 156.7 jit_solution(16340670958820460657)
XLA Ops:
  0.0 1.6 %reshape.15.conv_w = f32[9,2048]{1,0:T(8,128)} reshape(f32[3,3,2048]{2,1,0:T(4,128)} %param.7) | data formatting | bytes 147456 | tf_op jit(solution)/shard_map/reshape | solution.py:496
  1.6 1.1 sqrt_multiply_fusion
  2.7 0.7 reshape.18.gain
  3.4 0.7 reshape.17.decay_sec
  4.0 0.7 reshape.16.decay
  4.7 149.7 %shard_map.64 = bf16[256,2048]{1,0:T(8,128)(2,1)} custom-call(bf16[3,256,2048]{2,1,0:T(8,128)(2,1)} %qkv.1, f32[9,2048]{1,0:T(8,128)} %reshape.15.conv_w, f32[256,128]{1,0:T(8,128)} %reshape.16.decay, f32[256,128]{1,0:T(8,128)} %reshape.17.decay_sec, f32[256,128]{1,0:T(8,128)} %reshape.18.gain, f32[16,128]{1,0:T(8,128)} %bitcast.1, bf16[1024,2048]{1,0:T(8,128)(2,1)} %weight.1), custom_call_target="tpu_custom_call" | custom-call | flops 8589934592 | bytes 12582912 | tf_op jit(solution)/shard_map/pallas_call | solution.py:451
  154.4 2.3 %copy.8 = bf16[256,2048]{1,0:T(8,128)(2,1)} copy(bf16[256,2048]{1,0:T(8,128)(2,1)} %shard_map.64) | data formatting | bytes 2097152

commit v2 on v1

v2 whole, which is shorter than its diff:
```python
import functools

import jax
import jax.numpy as jnp
from jax import lax
from jax.experimental import pallas as pl
from jax.experimental.pallas import tpu as pltpu
from jax.sharding import PartitionSpec as P

MESH = pl.DeviceIdType.MESH
LANES = 128
HALO = 16


def token_parts(tok, nt):
    return 2 if tok % (2 * nt * HALO) == 0 else 1


def one_minus_exp(x):
    small = jnp.ones_like(x)
    for n in range(9, 1, -1):
        small = 1.0 - small * x * (1.0 / n)
    return jnp.where(x < 0.25, x * small, 1.0 - jnp.exp(-x))


def kernel(
    ns,
    nt,
    modes,
    qkv,
    conv_w,
    rate,
    residue,
    skip_row,
    weight,
    out,
    decay,
    decay_sec,
    gain,
    skip,
    halo,
    ext,
    prod,
    qf,
    mixed,
    wfull,
    state,
    other,
    total,
    totals,
    enter,
    stage,
    full,
    part,
    recv,
    own,
    halo_sem,
    w_sem,
    swap_sem,
    tot_send,
    tot_recv,
    s1_send,
    s1_recv,
    s2_send,
    s2_recv,
    s3_send,
    s3_recv,
    rs_send,
    rs_recv,
):
    nz = ns // 2
    tok = qkv.shape[1]
    ch = qkv.shape[2]
    groups = ch // LANES
    parts = token_parts(tok, nt)
    rows_part = tok // parts
    piece = rows_part // nt
    width = min(8, groups)
    halves = groups // width
    span = modes * width
    rows_w = weight.shape[0]
    cols = weight.shape[1]
    s = lax.axis_index("seq")
    t = lax.axis_index("tensor")
    z = s // 2
    c = s % 2
    mate = 2 * z + (1 - c)

    def dev(seq, ten):
        return (seq, ten)

    barrier = pltpu.get_barrier_semaphore()
    for d in range(1, ns):
        pl.semaphore_signal(barrier, inc=1, device_id=dev((s + d) % ns, t), device_id_type=MESH)
    for d in range(1, nt):
        pl.semaphore_signal(barrier, inc=1, device_id=dev(s, (t + d) % nt), device_id_type=MESH)
    pl.semaphore_wait(barrier, ns - 1 + nt - 1)

    halo_copy = pltpu.make_async_remote_copy(
        src_ref=qkv.at[:, pl.ds(tok - HALO, HALO), :],
        dst_ref=halo,
        send_sem=halo_sem.at[0],
        recv_sem=halo_sem.at[1],
        device_id=dev((s + 1) % ns, t),
        device_id_type=MESH,
    )

    @pl.when(s < ns - 1)
    def _():
        halo_copy.start()

    w_rows = pl.ds(pl.multiple_of(c * rows_w, rows_w), rows_w)
    w_remote = pltpu.make_async_remote_copy(
        src_ref=weight,
        dst_ref=wfull.at[w_rows, :],
        send_sem=w_sem.at[0],
        recv_sem=w_sem.at[1],
        device_id=dev(mate, t),
        device_id_type=MESH,
    )
    w_remote.start()
    w_local = pltpu.make_async_copy(weight, wfull.at[w_rows, :], w_sem.at[2])
    w_local.start()

    for g in range(groups):
        lanes = pl.ds(g * LANES, LANES)
        rows = pl.ds((g // width) * span + g % width, modes, stride=width)
        r = rate[:, lanes]
        decay[rows, :] = jnp.exp(-r)
        decay_sec[rows, :] = jnp.exp(-r * tok)
        gain[rows, :] = residue[:, lanes] * jnp.sqrt(one_minus_exp(2.0 * r))
        skip[g : g + 1, :] = skip_row[:, lanes]

    @pl.when(s == 0)
    def _():
        halo[...] = jnp.zeros_like(halo)

    @pl.when(s > 0)
    def _():
        halo_copy.wait_recv()

    def short(i, lanes):
        ext[i, 0:HALO, :] = halo[i, :, lanes].astype(jnp.float32)
        ext[i, HALO : HALO + tok, :] = qkv[i, :, lanes].astype(jnp.float32)
        taps = conv_w[i, :, lanes]
        return (
            taps[0:1] * ext[i, HALO : HALO + tok, :]
            + taps[1:2] * ext[i, HALO - 1 : HALO - 1 + tok, :]
            + taps[2:3] * ext[i, HALO - 2 : HALO - 2 + tok, :]
        )

    def mode_rows(ref, m, h):
        return ref[h * span + m * width : h * span + (m + 1) * width, :]

    def half_rows(h):
        return pl.ds(h * span, span)

    def tree(values):
        while len(values) > 1:
            values = [a + b for a, b in zip(values[::2], values[1::2])] + (
                [values[-1]] if len(values) % 2 else []
            )
        return values[0]

    def keys_values(h):
        for g in range(h * width, (h + 1) * width):
            lanes = pl.ds(g * LANES, LANES)
            prod[pl.ds(g, tok, stride=groups), :] = short(1, lanes) * short(2, lanes)

    def queries(h):
        for g in range(h * width, (h + 1) * width):
            lanes = pl.ds(g * LANES, LANES)
            qf[:, lanes] = short(0, lanes)

    def recur(h):
        skips = skip[h * width : (h + 1) * width, :]

        def step(i, states):
            rows = pl.ds(pl.multiple_of(i * groups + h * width, width), width)
            x = prod[rows, :]
            new = tuple(st * mode_rows(decay, m, h) + x for m, st in enumerate(states))
            terms = [st * mode_rows(gain, m, h) for m, st in enumerate(new)]
            prod[rows, :] = tree(terms) + skips * x
            return new

        states = lax.fori_loop(
            0,
            tok,
            step,
            tuple(jnp.zeros((width, LANES), jnp.float32) for _ in range(modes)),
            unroll=4,
        )
        for m in range(modes):
            state[h * span + m * width : h * span + (m + 1) * width, :] = states[m]

    def swap(h):
        return pltpu.make_async_remote_copy(
            src_ref=state.at[half_rows(h), :],
            dst_ref=other.at[half_rows(h), :],
            send_sem=swap_sem.at[0, h],
            recv_sem=swap_sem.at[1, h],
            device_id=dev(mate, t),
            device_id_type=MESH,
        )

    def tot_copy(h, target, source):
        return pltpu.make_async_remote_copy(
            src_ref=total.at[half_rows(h), :],
            dst_ref=totals.at[source, half_rows(h), :],
            send_sem=tot_send.at[h, target],
            recv_sem=tot_recv.at[h, source],
            device_id=dev(2 * target + c, t),
            device_id_type=MESH,
        )

    def send_totals(h):
        rows = half_rows(h)
        swap(h).wait_recv()

        @pl.when(c == 0)
        def _():
            total[rows, :] = (decay_sec[rows, :] * state[rows, :] + other[rows, :]).astype(
                total.dtype
            )

        @pl.when(c == 1)
        def _():
            total[rows, :] = (decay_sec[rows, :] * other[rows, :] + state[rows, :]).astype(
                total.dtype
            )

        for k in range(1, nz):

            @pl.when(k > z)
            def _(k=k):
                tot_copy(h, k, z).start()

    def entering(h):
        rows = half_rows(h)
        enter[rows, :] = jnp.zeros((span, LANES), jnp.float32)
        for k in range(nz - 1):

            @pl.when(k < z)
            def _(k=k):
                tot_copy(h, z, k).wait_recv()
                both = decay_sec[rows, :] * decay_sec[rows, :]
                enter[rows, :] = enter[rows, :] * both + totals[k, rows, :].astype(jnp.float32)

        @pl.when(c == 1)
        def _():
            enter[rows, :] = decay_sec[rows, :] * enter[rows, :] + other[rows, :]

    def fix(h):
        def step(i, carried):
            rows = pl.ds(pl.multiple_of(i * groups + h * width, width), width)
            prod[rows, :] = prod[rows, :] + tree(list(carried))
            return tuple(u * mode_rows(decay, m, h) for m, u in enumerate(carried))

        lax.fori_loop(
            0,
            tok,
            step,
            tuple(
                mode_rows(gain, m, h) * mode_rows(decay, m, h) * mode_rows(enter, m, h)
                for m in range(modes)
            ),
            unroll=4,
        )
        for g in range(h * width, (h + 1) * width):
            lanes = pl.ds(g * LANES, LANES)
            mixed[:, lanes] = (qf[:, lanes] * prod[pl.ds(g, tok, stride=groups), :]).astype(
                mixed.dtype
            )

    def share(p, index):
        return pl.ds(pl.multiple_of(p * rows_part + index * piece, piece), piece)

    def half_lanes(h):
        return pl.ds(h * width * LANES, width * LANES)

    def s1_copy(h, p, target, source):
        return pltpu.make_async_remote_copy(
            src_ref=mixed.at[share(p, target), half_lanes(h)],
            dst_ref=stage.at[p, source, :, half_lanes(h)],
            send_sem=s1_send.at[h, p, target],
            recv_sem=s1_recv.at[h, p, source],
            device_id=dev(s, target),
            device_id_type=MESH,
        )

    def s1_local(h, p):
        return pltpu.make_async_copy(
            mixed.at[share(p, t), half_lanes(h)],
            stage.at[p, t, :, half_lanes(h)],
            s1_recv.at[h, p, t],
        )

    def each_peer(body):
        def one(d, carry):
            body((t + d) % nt)
            return carry

        lax.fori_loop(1, nt, one, 0)

    def scatter(h):
        for p in range(parts):
            each_peer(lambda q: s1_copy(h, p, q, t).start())
            s1_local(h, p).start()

    def scattered(h, p, k):
        @pl.when(k == t)
        def _():
            s1_local(h, p).wait()

        @pl.when(k != t)
        def _():
            s1_copy(h, p, t, k).wait_recv()

    for h in range(halves):
        keys_values(h)
        if h > 0:
            send_totals(h - 1)
        recur(h)
        swap(h).start()
    queries(0)
    send_totals(halves - 1)
    for h in range(halves):
        if h > 0:
            queries(h)
        entering(h)
        fix(h)
        scatter(h)

    def s2_copy(h, p, target, source):
        return pltpu.make_async_remote_copy(
            src_ref=stage.at[p, target, :, half_lanes(h)],
            dst_ref=full.at[source, share(p, t), half_lanes(h)],
            send_sem=s2_send.at[h, p, target],
            recv_sem=s2_recv.at[h, p, source],
            device_id=dev(2 * target + c, t),
            device_id_type=MESH,
        )

    def s2_local(h, p):
        return pltpu.make_async_copy(
            stage.at[p, z, :, half_lanes(h)],
            full.at[z, share(p, t), half_lanes(h)],
            s2_recv.at[h, p, z],
        )

    candidates = 2 * (nz - 1) * parts

    def each_plane(f, body):
        p = f % parts
        e = f // parts
        d = nz - 1 - e // 2
        k = z + d * (1 - 2 * (e % 2))

        @pl.when((k >= 0) & (k < nz))
        def _():
            body(k, p)

    def loop_planes(body):
        def one(f, carry):
            each_plane(f, body)
            return carry

        lax.fori_loop(0, candidates, one, 0)

    for h in range(halves):

        def go(k, p, h=h):
            scattered(h, p, k)
            s2_copy(h, p, k, z).start()

        loop_planes(go)
        for p in range(parts):
            scattered(h, p, z)
            s2_local(h, p).start()

    def s3_copy(target, source, k, p):
        rows = full.at[k, share(p, source), :]
        return pltpu.make_async_remote_copy(
            src_ref=rows,
            dst_ref=rows,
            send_sem=s3_send.at[k * parts + p, target],
            recv_sem=s3_recv.at[k * parts + p, source],
            device_id=dev(s, target),
            device_id_type=MESH,
        )

    def spread(k, p):
        each_peer(lambda q: s3_copy(q, t, k, p).start())

    def spread_received(k, p):
        for h in range(halves):
            s2_copy(h, p, z, k).wait_recv()
        spread(k, p)

    def gathered(k, p):
        each_peer(lambda q: s3_copy(t, q, k, p).wait_recv())

    tile = min(512, cols)

    def part_rows(p):
        return pl.ds(pl.multiple_of(p * rows_part, rows_part), rows_part)

    def product(k, p, store):
        def one(n, carry):
            lanes = pl.ds(pl.multiple_of(n * tile, tile), tile)
            store(
                lanes,
                jnp.dot(
                    full[k, part_rows(p), :],
                    wfull[:, lanes],
                    preferred_element_type=jnp.float32,
                ),
            )
            return carry

        lax.fori_loop(0, cols // tile, one, 0)

    def rs_copy(k, p, slot, target):
        return pltpu.make_async_remote_copy(
            src_ref=part.at[k, part_rows(p), :],
            dst_ref=recv.at[slot, part_rows(p), :],
            send_sem=rs_send.at[k, p],
            recv_sem=rs_recv.at[slot, p],
            device_id=dev(2 * target + c, t),
            device_id_type=MESH,
        )

    def rs_wait(slot, p):
        rs_copy(z, p, slot, z).wait_recv()

    def contribute(k, p):
        gathered(k, p)
        rows = part_rows(p)

        def fresh(lanes, value):
            part[k, rows, lanes] = value.astype(part.dtype)

        def added(lanes, value):
            part[k, rows, lanes] = (value + recv[k, rows, lanes].astype(jnp.float32)).astype(
                part.dtype
            )

        first = ((k > z) & (z == 0)) | ((k < z) & (z == nz - 1))

        @pl.when(first)
        def _():
            product(k, p, fresh)

        @pl.when(jnp.logical_not(first))
        def _():
            rs_wait(k, p)
            product(k, p, added)

        @pl.when(k > z)
        def _():
            rs_copy(k, p, k, z + 1).start()

        @pl.when(k < z - 1)
        def _():
            rs_copy(k, p, k, z - 1).start()

        @pl.when(k == z - 1)
        def _():
            rs_copy(k, p, nz, z - 1).start()

    lead = parts
    for f in range(lead):
        each_plane(f, spread_received)
    for p in range(parts):
        for h in range(halves):
            s2_local(h, p).wait()
        spread(z, p)
    w_local.wait()
    w_remote.wait_recv()

    def one_plane(f, carry):
        @pl.when(f + lead < candidates)
        def _():
            each_plane(f + lead, spread_received)

        each_plane(f, contribute)
        return carry

    lax.fori_loop(0, candidates, one_plane, 0)

    for p in range(parts):
        gathered(z, p)

        def keep_own(lanes, value, p=p):
            own[part_rows(p), lanes] = value

        product(z, p, keep_own)

    for p in range(parts):
        rows = part_rows(p)

        @pl.when(z > 0)
        def _(p=p, rows=rows):
            rs_wait(z, p)
            own[rows, :] += recv[z, rows, :].astype(jnp.float32)

        @pl.when(z < nz - 1)
        def _(p=p, rows=rows):
            rs_wait(nz, p)
            own[rows, :] += recv[nz, rows, :].astype(jnp.float32)

        out[rows, :] = own[rows, :].astype(out.dtype)

    @pl.when(s < ns - 1)
    def _():
        halo_copy.wait_send()

    w_remote.wait_send()
    for h in range(halves):
        swap(h).wait_send()
        for k in range(1, nz):

            @pl.when(k > z)
            def _(k=k, h=h):
                tot_copy(h, k, z).wait_send()

        for p in range(parts):
            each_peer(lambda q, h=h, p=p: s1_copy(h, p, q, t).wait_send())
        loop_planes(lambda k, p, h=h: s2_copy(h, p, k, z).wait_send())

    def all_sent(k, p):
        each_peer(lambda q: s3_copy(q, t, k, p).wait_send())

    for p in range(parts):
        all_sent(z, p)
    loop_planes(all_sent)
    loop_planes(lambda k, p: rs_copy(k, p, k, z).wait_send())


def local(ns, nt, qkv, conv_weight, decay_rate, residue, skip_gain, out_weight):
    tok, ch = qkv.shape[1], qkv.shape[2]
    modes = decay_rate.shape[0]
    groups = ch // LANES
    nz = ns // 2
    cols = out_weight.shape[1]
    rows = modes * groups
    parts = token_parts(tok, nt)
    halves = groups // min(8, groups)
    vmem = pl.BlockSpec(memory_space=pltpu.VMEM)
    f32, bf16 = jnp.float32, jnp.bfloat16
    dma = pltpu.SemaphoreType.DMA
    return pl.pallas_call(
        functools.partial(kernel, ns, nt, modes),
        out_shape=jax.ShapeDtypeStruct((tok, cols), bf16),
        in_specs=[vmem] * 5 + [pl.BlockSpec(memory_space=pl.ANY)],
        out_specs=vmem,
        scratch_shapes=[
            pltpu.VMEM((rows, LANES), f32),
            pltpu.VMEM((rows, LANES), f32),
            pltpu.VMEM((rows, LANES), f32),
            pltpu.VMEM((groups, LANES), f32),
            pltpu.VMEM((3, HALO, ch), bf16),
            pltpu.VMEM((3, HALO + tok, LANES), f32),
            pltpu.VMEM((tok * groups, LANES), f32),
            pltpu.VMEM((tok, ch), f32),
            pltpu.VMEM((tok, ch), bf16),
            pltpu.VMEM((ch, cols), bf16),
            pltpu.VMEM((rows, LANES), f32),
            pltpu.VMEM((rows, LANES), f32),
            pltpu.VMEM((rows, LANES), bf16),
            pltpu.VMEM((nz, rows, LANES), bf16),
            pltpu.VMEM((rows, LANES), f32),
            pltpu.VMEM((parts, nt, tok // parts // nt, ch), bf16),
            pltpu.VMEM((nz, tok, ch), bf16),
            pltpu.VMEM((nz, tok, cols), bf16),
            pltpu.VMEM((nz + 1, tok, cols), bf16),
            pltpu.VMEM((tok, cols), f32),
            dma((2,)),
            dma((3,)),
            dma((2, halves)),
            dma((halves, nz)),
            dma((halves, nz)),
            dma((halves, parts, nt)),
            dma((halves, parts, nt)),
            dma((halves, parts, nz)),
            dma((halves, parts, nz)),
            dma((nz * parts, nt)),
            dma((nz * parts, nt)),
            dma((nz, parts)),
            dma((nz + 1, parts)),
        ],
        compiler_params=pltpu.CompilerParams(
            collective_id=0, has_side_effects=True, vmem_limit_bytes=56 * 1024 * 1024
        ),
        cost_estimate=pl.CostEstimate(
            flops=2 * tok * nz * ch * cols, bytes_accessed=12 * 1024 * 1024, transcendentals=0
        ),
    )(
        qkv,
        conv_weight,
        decay_rate,
        residue,
        skip_gain.reshape(1, ch),
        out_weight,
    )


def solution(mesh):
    return jax.shard_map(
        functools.partial(local, mesh.shape["seq"], mesh.shape["tensor"]),
        mesh=mesh,
        in_specs=(
            P(None, "seq", "tensor"),
            P(None, None, "tensor"),
            P(None, "tensor"),
            P(None, "tensor"),
            P("tensor"),
            P("seq", "tensor"),
        ),
        out_specs=P("seq", "tensor"),
        check_vma=False,
    )
```

time: 157 us -> 132 us (0.84)
  the two profiles are of different devices: /device:TPU:0 before, /device:TPU:16 now
where the time goes in v2:
time: 132 us; the launch traced here: 131 us
  Pallas kernels  129 us (98%)
  local copies, waits for them, and re-layouts  2.3 us (2%)
    pallas_call x1, Pallas kernels, local(): pl.pallas_call(functools.partial(kernel, ns, nt, modes), out_shape=jax.Sh...  129 us

profile of v2, /device:TPU:16, one launch (start us, length us, event | category | flops | bytes accessed | tf_op | source)
XLA Modules:
  0.0 131.4 jit_solution(16477394881022441357)
XLA Ops:
  0.0 129.1 %shard_map.64 = bf16[256,2048]{1,0:T(8,128)(2,1)} custom-call(bf16[3,256,2048]{2,1,0:T(8,128)(2,1)} %qkv.1, f32[3,3,2048]{2,1,0:T(4,128)} %conv_w.1, f32[16,2048]{1,0:T(8,128)} %rate.1, f32[16,2048]{1,0:T(8,128)} %residue.1, f32[1,2048]{1,0:T(1,128)} %bitcast.1, bf16[1024,2048]{1,0:T(8,128)(2,1)} %weight.1), custom_call_target="tpu_custom_call" | custom-call | flops 8589934592 | bytes 12582912 | tf_op jit(solution)/shard_map/pallas_call | solution.py:552
  129.1 2.3 %copy.8 = bf16[256,2048]{1,0:T(8,128)(2,1)} copy(bf16[256,2048]{1,0:T(8,128)(2,1)} %shard_map.64) | data formatting | bytes 2097152

commit v3 on v2

--- a/solution.py
+++ b/solution.py
@@ -94,7 +94,6 @@
         pl.semaphore_signal(barrier, inc=1, device_id=dev((s + d) % ns, t), device_id_type=MESH)
     for d in range(1, nt):
         pl.semaphore_signal(barrier, inc=1, device_id=dev(s, (t + d) % nt), device_id_type=MESH)
-    pl.semaphore_wait(barrier, ns - 1 + nt - 1)
 
     halo_copy = pltpu.make_async_remote_copy(
         src_ref=qkv.at[:, pl.ds(tok - HALO, HALO), :],
@@ -104,10 +103,6 @@
         device_id=dev((s + 1) % ns, t),
         device_id_type=MESH,
     )
-
-    @pl.when(s < ns - 1)
-    def _():
-        halo_copy.start()
 
     w_rows = pl.ds(pl.multiple_of(c * rows_w, rows_w), rows_w)
     w_remote = pltpu.make_async_remote_copy(
@@ -118,36 +113,20 @@
         device_id=dev(mate, t),
         device_id_type=MESH,
     )
-    w_remote.start()
     w_local = pltpu.make_async_copy(weight, wfull.at[w_rows, :], w_sem.at[2])
-    w_local.start()
-
-    for g in range(groups):
-        lanes = pl.ds(g * LANES, LANES)
-        rows = pl.ds((g // width) * span + g % width, modes, stride=width)
-        r = rate[:, lanes]
-        decay[rows, :] = jnp.exp(-r)
-        decay_sec[rows, :] = jnp.exp(-r * tok)
-        gain[rows, :] = residue[:, lanes] * jnp.sqrt(one_minus_exp(2.0 * r))
-        skip[g : g + 1, :] = skip_row[:, lanes]
-
-    @pl.when(s == 0)
-    def _():
-        halo[...] = jnp.zeros_like(halo)
-
-    @pl.when(s > 0)
-    def _():
-        halo_copy.wait_recv()
-
-    def short(i, lanes):
-        ext[i, 0:HALO, :] = halo[i, :, lanes].astype(jnp.float32)
-        ext[i, HALO : HALO + tok, :] = qkv[i, :, lanes].astype(jnp.float32)
+
+    def short(i, lanes, head, count):
+        ext[i, 0:HALO, :] = head
+        ext[i, HALO : HALO + count, :] = qkv[i, 0:count, lanes].astype(jnp.float32)
         taps = conv_w[i, :, lanes]
         return (
-            taps[0:1] * ext[i, HALO : HALO + tok, :]
-            + taps[1:2] * ext[i, HALO - 1 : HALO - 1 + tok, :]
-            + taps[2:3] * ext[i, HALO - 2 : HALO - 2 + tok, :]
-        )
+            taps[0:1] * ext[i, HALO : HALO + count, :]
+            + taps[1:2] * ext[i, HALO - 1 : HALO - 1 + count, :]
+            + taps[2:3] * ext[i, HALO - 2 : HALO - 2 + count, :]
+        )
+
+    def before(i, lanes):
+        return halo[i, :, lanes].astype(jnp.float32)
 
     def mode_rows(ref, m, h):
         return ref[h * span + m * width : h * span + (m + 1) * width, :]
@@ -163,14 +142,24 @@
         return values[0]
 
     def keys_values(h):
+        zero = jnp.zeros((HALO, LANES), jnp.float32)
         for g in range(h * width, (h + 1) * width):
             lanes = pl.ds(g * LANES, LANES)
-            prod[pl.ds(g, tok, stride=groups), :] = short(1, lanes) * short(2, lanes)
+            prod[pl.ds(g, tok, stride=groups), :] = short(1, lanes, zero, tok) * short(
+                2, lanes, zero, tok
+            )
+
+    def first_rows(h):
+        for g in range(h * width, (h + 1) * width):
+            lanes = pl.ds(g * LANES, LANES)
+            prod[pl.ds(g, HALO, stride=groups), :] = short(
+                1, lanes, before(1, lanes), HALO
+            ) * short(2, lanes, before(2, lanes), HALO)
 
     def queries(h):
         for g in range(h * width, (h + 1) * width):
             lanes = pl.ds(g * LANES, LANES)
-            qf[:, lanes] = short(0, lanes)
+            qf[:, lanes] = short(0, lanes, before(0, lanes), tok)
 
     def recur(h):
         skips = skip[h * width : (h + 1) * width, :]
@@ -316,21 +305,6 @@
         def _():
             s1_copy(h, p, t, k).wait_recv()
 
-    for h in range(halves):
-        keys_values(h)
-        if h > 0:
-            send_totals(h - 1)
-        recur(h)
-        swap(h).start()
-    queries(0)
-    send_totals(halves - 1)
-    for h in range(halves):
-        if h > 0:
-            queries(h)
-        entering(h)
-        fix(h)
-        scatter(h)
-
     def s2_copy(h, p, target, source):
         return pltpu.make_async_remote_copy(
             src_ref=stage.at[p, target, :, half_lanes(h)],
@@ -351,10 +325,9 @@
     candidates = 2 * (nz - 1) * parts
 
     def each_plane(f, body):
-        p = f % parts
-        e = f // parts
-        d = nz - 1 - e // 2
-        k = z + d * (1 - 2 * (e % 2))
+        p = (f // 2) % parts
+        d = nz - 1 - f // (2 * parts)
+        k = z + d * (1 - 2 * (f % 2))
 
         @pl.when((k >= 0) & (k < nz))
         def _():
@@ -367,9 +340,8 @@
 
         lax.fori_loop(0, candidates, one, 0)
 
-    for h in range(halves):
-
-        def go(k, p, h=h):
+    def to_planes(h):
+        def go(k, p):
             scattered(h, p, k)
             s2_copy(h, p, k, z).start()
 
@@ -377,6 +349,55 @@
         for p in range(parts):
             scattered(h, p, z)
             s2_local(h, p).start()
+
+    for g in range(groups):
+        lanes = pl.ds(g * LANES, LANES)
+        rows = pl.ds((g // width) * span + g % width, modes, stride=width)
+        r = rate[:, lanes]
+        decay[rows, :] = jnp.exp(-r)
+        decay_sec[rows, :] = jnp.exp(-r * tok)
+        gain[rows, :] = residue[:, lanes] * jnp.sqrt(one_minus_exp(2.0 * r))
+        skip[g : g + 1, :] = skip_row[:, lanes]
+
+    keys_values(0)
+    pl.semaphore_wait(barrier, ns - 1 + nt - 1)
+
+    @pl.when(s < ns - 1)
+    def _():
+        halo_copy.start()
+
+    w_remote.start()
+    w_local.start()
+
+    @pl.when(s == 0)
+    def _():
+        halo[...] = jnp.zeros_like(halo)
+
+    @pl.when(s > 0)
+    def _():
+        halo_copy.wait_recv()
+
+    first_rows(0)
+    recur(0)
+    swap(0).start()
+    for h in range(halves):
+        if h + 1 < halves:
+            keys_values(h + 1)
+            first_rows(h + 1)
+        else:
+            queries(h)
+        send_totals(h)
+        if h > 0:
+            to_planes(h - 1)
+        if h + 1 < halves:
+            queries(h)
+        entering(h)
+        fix(h)
+        scatter(h)
+        if h + 1 < halves:
+            recur(h + 1)
+            swap(h + 1).start()
+    to_planes(halves - 1)
 
     def s3_copy(target, source, k, p):
         rows = full.at[k, share(p, source), :]
@@ -468,7 +489,7 @@
         def _():
             rs_copy(k, p, nz, z - 1).start()
 
-    lead = parts
+    lead = 2
     for f in range(lead):
         each_plane(f, spread_received)
     for p in range(parts):

time: 132 us -> 132 us (level)
  no operation moved by 1% of the time
where the time goes in v3:
time: 132 us; the launch traced here: 131 us
  Pallas kernels  129 us (98%)
  local copies, waits for them, and re-layouts  2.3 us (2%)
    pallas_call x1, Pallas kernels, local(): pl.pallas_call(functools.partial(kernel, ns, nt, modes), out_shape=jax.Sh...  129 us

profile of v3, /device:TPU:16, one launch (start us, length us, event | category | flops | bytes accessed | tf_op | source)
XLA Modules:
  0.0 131.4 jit_solution(6633795375643254801)
XLA Ops:
  0.0 129.1 %shard_map.64 = bf16[256,2048]{1,0:T(8,128)(2,1)} custom-call(bf16[3,256,2048]{2,1,0:T(8,128)(2,1)} %qkv.1, f32[3,3,2048]{2,1,0:T(4,128)} %conv_w.1, f32[16,2048]{1,0:T(8,128)} %rate.1, f32[16,2048]{1,0:T(8,128)} %residue.1, f32[1,2048]{1,0:T(1,128)} %bitcast.1, bf16[1024,2048]{1,0:T(8,128)(2,1)} %weight.1), custom_call_target="tpu_custom_call" | custom-call | flops 8589934592 | bytes 12582912 | tf_op jit(solution)/shard_map/pallas_call | solution.py:573
  129.1 2.3 %copy.8 = bf16[256,2048]{1,0:T(8,128)(2,1)} copy(bf16[256,2048]{1,0:T(8,128)(2,1)} %shard_map.64) | data formatting | bytes 2097152

commit v4 on v3

--- a/solution.py
+++ b/solution.py
@@ -366,9 +366,6 @@
     def _():
         halo_copy.start()
 
-    w_remote.start()
-    w_local.start()
-
     @pl.when(s == 0)
     def _():
         halo[...] = jnp.zeros_like(halo)
@@ -378,26 +375,25 @@
         halo_copy.wait_recv()
 
     first_rows(0)
-    recur(0)
-    swap(0).start()
     for h in range(halves):
-        if h + 1 < halves:
-            keys_values(h + 1)
-            first_rows(h + 1)
-        else:
-            queries(h)
-        send_totals(h)
         if h > 0:
-            to_planes(h - 1)
-        if h + 1 < halves:
+            keys_values(h)
+            first_rows(h)
+            send_totals(h - 1)
+        recur(h)
+        swap(h).start()
+    queries(0)
+    send_totals(halves - 1)
+    w_remote.start()
+    w_local.start()
+    for h in range(halves):
+        if h > 0:
             queries(h)
         entering(h)
         fix(h)
         scatter(h)
-        if h + 1 < halves:
-            recur(h + 1)
-            swap(h + 1).start()
-    to_planes(halves - 1)
+    for h in range(halves):
+        to_planes(h)
 
     def s3_copy(target, source, k, p):
         rows = full.at[k, share(p, source), :]

time: 132 us -> 123 us (0.932)
  the two profiles are of different devices: /device:TPU:16 before, /device:TPU:0 now
where the time goes in v4:
time: 123 us; the launch traced here: 121 us
  Pallas kernels  119 us (97%)
  local copies, waits for them, and re-layouts  2.3 us (2%)
    pallas_call x1, Pallas kernels, local(): pl.pallas_call(functools.partial(kernel, ns, nt, modes), out_shape=jax.Sh...  119 us

profile of v4, /device:TPU:0, one launch (start us, length us, event | category | flops | bytes accessed | tf_op | source)
XLA Modules:
  0.0 121.3 jit_solution(8504883394891043809)
XLA Ops:
  0.0 119.0 %shard_map.64 = bf16[256,2048]{1,0:T(8,128)(2,1)} custom-call(bf16[3,256,2048]{2,1,0:T(8,128)(2,1)} %qkv.1, f32[3,3,2048]{2,1,0:T(4,128)} %conv_w.1, f32[16,2048]{1,0:T(8,128)} %rate.1, f32[16,2048]{1,0:T(8,128)} %residue.1, f32[1,2048]{1,0:T(1,128)} %bitcast.1, bf16[1024,2048]{1,0:T(8,128)(2,1)} %weight.1), custom_call_target="tpu_custom_call" | custom-call | flops 8589934592 | bytes 12582912 | tf_op jit(solution)/shard_map/pallas_call | solution.py:569
  119.0 2.3 %copy.8 = bf16[256,2048]{1,0:T(8,128)(2,1)} copy(bf16[256,2048]{1,0:T(8,128)(2,1)} %shard_map.64) | data formatting | bytes 2097152

commit v5 on v4

--- a/solution.py
+++ b/solution.py
@@ -13,7 +13,7 @@
 
 
 def token_parts(tok, nt):
-    return 2 if tok % (2 * nt * HALO) == 0 else 1
+    return next(n for n in (4, 2, 1) if tok % (n * nt * HALO) == 0)
 
 
 def one_minus_exp(x):
@@ -454,24 +454,22 @@
         gathered(k, p)
         rows = part_rows(p)
 
-        def fresh(lanes, value):
-            part[k, rows, lanes] = value.astype(part.dtype)
-
-        def added(lanes, value):
-            part[k, rows, lanes] = (value + recv[k, rows, lanes].astype(jnp.float32)).astype(
+        def hold(lanes, value):
+            own[rows, lanes] = value
+
+        product(k, p, hold)
+        first = ((k > z) & (z == 0)) | ((k < z) & (z == nz - 1))
+
+        @pl.when(first)
+        def _():
+            part[k, rows, :] = own[rows, :].astype(part.dtype)
+
+        @pl.when(jnp.logical_not(first))
+        def _():
+            rs_wait(k, p)
+            part[k, rows, :] = (own[rows, :] + recv[k, rows, :].astype(jnp.float32)).astype(
                 part.dtype
             )
-
-        first = ((k > z) & (z == 0)) | ((k < z) & (z == nz - 1))
-
-        @pl.when(first)
-        def _():
-            product(k, p, fresh)
-
-        @pl.when(jnp.logical_not(first))
-        def _():
-            rs_wait(k, p)
-            product(k, p, added)
 
         @pl.when(k > z)
         def _():

time: 123 us -> 126 us (1.024)
  the two profiles are of different devices: /device:TPU:0 before, /device:TPU:12 now
where the time goes in v5:
time: 126 us
  Pallas kernels  123 us (98%)
  local copies, waits for them, and re-layouts  2.3 us (2%)
    pallas_call x1, Pallas kernels, local(): pl.pallas_call(functools.partial(kernel, ns, nt, modes), out_shape=jax.Sh...  123 us

profile of v5, /device:TPU:12, one launch (start us, length us, event | category | flops | bytes accessed | tf_op | source)
XLA Modules:
  0.0 125.7 jit_solution(2067675433093664860)
XLA Ops:
  0.0 123.4 %shard_map.64 = bf16[256,2048]{1,0:T(8,128)(2,1)} custom-call(bf16[3,256,2048]{2,1,0:T(8,128)(2,1)} %qkv.1, f32[3,3,2048]{2,1,0:T(4,128)} %conv_w.1, f32[16,2048]{1,0:T(8,128)} %rate.1, f32[16,2048]{1,0:T(8,128)} %residue.1, f32[1,2048]{1,0:T(1,128)} %bitcast.1, bf16[1024,2048]{1,0:T(8,128)(2,1)} %weight.1), custom_call_target="tpu_custom_call" | custom-call | flops 8589934592 | bytes 12582912 | tf_op jit(solution)/shard_map/pallas_call | solution.py:567
  123.4 2.3 %copy.8 = bf16[256,2048]{1,0:T(8,128)(2,1)} copy(bf16[256,2048]{1,0:T(8,128)(2,1)} %shard_map.64) | data formatting | bytes 2097152
